TPU v7x, 512 devices: a whole 4x8x8 slice. The times are simulated.
512 devices in a mesh: row: 16 (over y, x_lo), col: 16 (over z, core), lag: 2 (over x_hi).
Axes of the slice: x: 4 (x_hi: 2, x_lo: 2; x = x_hi * 2 + x_lo), y: 8, z: 8, core: 2. Of those that a mesh axis runs over, the one named last changes fastest.
Arguments:
- trajectories: bfloat16 [16384, 4096], P(('row', 'col'), 'lag'), may hold values from -6 to 6
- pair_live: int32 [16, 16], replicated, may hold values from 0 to 1, as said below
Outputs:
- gram: bfloat16 [16384, 16384], P(('row', 'lag'), 'col')
Inputs may be any that keep to these rules, and one draw needn't show every extreme that they name: `pair_live`: Symmetric, with every diagonal entry 1.
All inputs are finite; a program needn't handle non-finite values.
Results may differ from a plain program's by a relative error of at most 0.0015.
Values may be sent and summed in bfloat16 or wider, within the bound.
No kernel may reach another device: no remote copies, remote signals or barrier semaphores. Data moves between devices by JAX's collectives and lax.ppermute only.
A program may use at most 64 MiB of HBM per device.

v0:
```python
import jax
import jax.numpy as jnp
from jax import lax
from jax.sharding import PartitionSpec as P


def from_root(value, axis, source):
    kept = jnp.where(lax.axis_index(axis) == source, value, 0).astype(value.dtype)
    return lax.psum(kept, axis)


def pair_distance(left, right, left_norm, right_norm):
    inner = lax.dot_general(
        left, right, (((1,), (1,)), ((), ())), preferred_element_type=jnp.float32
    )
    return left_norm[:, None] + right_norm[None, :] - 2.0 * inner


def squares(block):
    return jnp.sum(jnp.square(block.astype(jnp.float32)), axis=1)


def on_device(trajectories, pair_live):
    row_block = lax.all_gather(trajectories, "col", axis=0, tiled=True)
    col_block = from_root(row_block, "row", lax.axis_index("col"))
    live = pair_live[lax.axis_index("row"), lax.axis_index("col")]
    samples = trajectories.shape[1] * lax.axis_size("lag")
    row_norm = squares(row_block)
    col_norm = squares(col_block)
    dist = lax.psum_scatter(
        pair_distance(row_block, col_block, row_norm, col_norm),
        "lag",
        scatter_dimension=0,
        tiled=True,
    )
    gram = jnp.exp(-2.0 * dist / samples) * live.astype(jnp.float32)
    return gram.astype(jnp.bfloat16)


def solution(mesh):
    return jax.shard_map(
        on_device,
        mesh=mesh,
        in_specs=(P(("row", "col"), "lag"), P()),
        out_specs=P(("row", "lag"), "col"),
        check_vma=False,
    )
```

profile of v0, /device:TPU:1, one launch (start us, length us, event | category | flops | bytes accessed | tf_op | source)
XLA Modules:
  0.0 353.9 jit_solution(6171792190010791576)
XLA Ops:
  6.5 0.0 all-gather.2.cloned.1.call-start
  6.5 0.7 all-gather.2.cloned.1.call-update
  7.3 0.0 all-reduce.2.cloned.1.call-start
  7.3 53.8 %all-gather.2.cloned.1.call-done = bf16[1024,2048]{1,0:T(8,128)(2,1)} async-done(((bf16[64,2048]{1,0:T(8,128)(2,1)}), bf16[1024,2048]{1,0:T(8,128)(2,1)}) %all-gather.2.cloned.1.call-update) | async-done | bytes 4194320 | tf_op jit(solution)/shard_map/all_gather | solution.py:24
  61.1 2.3 broadcast_select_fusion
  63.3 0.0 all-reduce.2.cloned.1.call-update
  63.4 0.0 reduce-scatter.2.cloned.1.call-start
  63.4 3.1 multiply_reduce_fusion.1
  66.5 200.5 %all-reduce.2.cloned.1.call-done = bf16[1024,2048]{1,0:T(8,128)(2,1)} async-done(((bf16[1024,2048]{1,0:T(8,128)(2,1)}), bf16[1024,2048]{1,0:T(8,128)(2,1)}) %all-reduce.2.cloned.1.call-update) | async-done | bytes 4194320 | tf_op jit(solution)/shard_map/psum | solution.py:9
  267.0 0.0 copy-start
  267.0 3.2 multiply_reduce_fusion
  270.2 0.2 copy-done
  270.5 8.3 %bitcast_subtract_fusion = f32[1024,1024]{0,1:T(8,128)} fusion(bf16[1024,2048]{1,0:T(8,128)(2,1)} %all-reduce.2.cloned.1.call-done, bf16[1024,2048]{1,0:T(8,128)(2,1)S(1)} %copy-done, f32[1024]{0:T(1024)S(1)} %multiply_reduce_fusion, f32[1024]{0:T(1024)S(1)} %multiply_reduce_fusion.1), kind=kOutput, calls=%fused_computation.2 | convolution fusion | flops 4298113024 | bytes 12591104 | tf_op jit(solution)/shard_map/dot_general | solution.py:13
  278.8 0.0 reduce-scatter.2.cloned.1.call-update
  278.8 1.3 dynamic_slice.3
  280.7 63.4 %reduce-scatter.2.cloned.1.call-done = f32[512,1024]{0,1:T(8,128)} async-done(((f32[1024,1024]{0,1:T(8,128)}), f32[512,1024]{0,1:T(8,128)}) %reduce-scatter.2.cloned.1.call-update) | async-done | bytes 2097168 | tf_op jit(solution)/shard_map/reduce_scatter | solution.py:30
  344.1 1.9 multiply_convert_fusion
  346.0 1.3 copy.3
Async XLA Ops:
  6.5 54.6 %all-gather.2.cloned.1.call-start = ((), (), s32[]{:S(2)}) async-start(), calls=%async_computation.1 | async-start | bytes 4456448 | tf_op jit(solution)/shard_map/all_gather | solution.py:24
  7.3 259.8 %all-reduce.2.cloned.1.call-start = ((), (), s32[]{:S(2)}) async-start(), calls=%async_computation.2 | async-start | bytes 8388608 | tf_op jit(solution)/shard_map/psum | solution.py:9
  63.4 280.7 %reduce-scatter.2.cloned.1.call-start = ((), (), s32[]{:S(2)}) async-start(), calls=%async_computation.3 | async-start | bytes 6291456 | tf_op jit(solution)/shard_map/reduce_scatter | solution.py:30
  267.0 3.4 copy-start
Sparse Core Ops, SparseCore 0:
  9.5 51.5 all-gather.1
  64.0 202.9 all-reduce.1
  278.9 65.1 reduce-scatter.1
where the time goes:
time: 354 us
  waiting for transfers between devices  318 us (90%)
  between operations  13.8 us (4%)
  other arithmetic  10.5 us (3%)
  matrix products  8.28 us (2%)
    psum x1, waiting for transfers between devices, from_root(): return lax.psum(kept, axis)  201 us
    reduce_scatter x1, waiting for transfers between devices, on_device(): lax.psum_scatter(pair_distance(row_block, col_block, row_norm, col_norm),...  63.4 us
    all_gather x1, waiting for transfers between devices, on_device(): row_block = lax.all_gather(trajectories, 'col', axis=0, tiled=True)  53.8 us
    dot_general x1, matrix products, pair_distance(): lax.dot_general(left, right, (((1,), (1,)), ((), ())), preferred_element_...  8.28 us
  transfers between devices with their start and end apart: 3, of which 3 were waited for; matrix products, arithmetic and copies ran while one was open for 1% of the time, Pallas kernels for 0%

commit v1 on v0

--- a/solution.py
+++ b/solution.py
@@ -21,7 +21,10 @@
 
 
 def on_device(trajectories, pair_live):
-    row_block = lax.all_gather(trajectories, "col", axis=0, tiled=True)
+    size = lax.axis_size("col")
+    blocks = jnp.stack([trajectories for _ in range(size)])
+    blocks = lax.all_to_all(blocks, "col", split_axis=0, concat_axis=0)
+    row_block = jnp.concatenate(blocks, axis=0)
     col_block = from_root(row_block, "row", lax.axis_index("col"))
     live = pair_live[lax.axis_index("row"), lax.axis_index("col")]
     samples = trajectories.shape[1] * lax.axis_size("lag")

time: 354 us -> 410 us (1.16)
  waiting for transfers between devices: 318 us -> 357 us
  starting transfers between devices: 0.08 us -> 11.9 us
    all_to_all x0 -> x1, waiting for transfers between devices: none -> 93.5 us  [on_device(): blocks = lax.all_to_all(blocks, 'col', split_axis=0, concat_axis=0)]
    all_gather x1 -> x0, waiting for transfers between devices: 53.8 us -> none  [on_device(): row_block = lax.all_gather(trajectories, 'col', axis=0, tiled=True)]
    all_to_all x0 -> x1, starting transfers between devices: none -> 11.8 us  [on_device(): blocks = lax.all_to_all(blocks, 'col', split_axis=0, concat_axis=0)]
where the time goes in v1:
time: 410 us
  waiting for transfers between devices  357 us (87%)
  between operations  14.1 us (3%)
  other arithmetic  12.6 us (3%)
  starting transfers between devices  11.9 us (3%)
  matrix products  8.29 us (2%)
  local copies, waits for them, and re-layouts  6.33 us (2%)
    psum x1, waiting for transfers between devices, from_root(): return lax.psum(kept, axis)  200 us
    all_to_all x1, waiting for transfers between devices, on_device(): blocks = lax.all_to_all(blocks, 'col', split_axis=0, concat_axis=0)  93.5 us
    reduce_scatter x1, waiting for transfers between devices, on_device(): lax.psum_scatter(pair_distance(row_block, col_block, row_norm, col_norm),...  63.4 us
    all_to_all x1, starting transfers between devices, on_device(): blocks = lax.all_to_all(blocks, 'col', split_axis=0, concat_axis=0)  11.8 us
    dot_general x1, matrix products, pair_distance(): lax.dot_general(left, right, (((1,), (1,)), ((), ())), preferred_element_...  8.29 us
  transfers between devices with their start and end apart: 3, of which 3 were waited for; matrix products, arithmetic and copies ran while one was open for 1% of the time, Pallas kernels for 0%

profile of v1, /device:TPU:1, one launch (start us, length us, event | category | flops | bytes accessed | tf_op | source)
XLA Modules:
  0.0 410.1 jit_solution(15486271560886033314)
XLA Ops:
  6.5 3.4 stack.2
  10.0 11.8 %all-to-all-start = ((bf16[16,64,2048]{2,1,0:T(8,128)(2,1)}), bf16[16,64,2048]{2,1,0:T(8,128)(2,1)}, u32[]{:S(2)}, u32[]{:S(2)}) async-start(bf16[16,64,2048]{2,1,0:T(8,128)(2,1)} %stack.2), calls=%async_computation | async-start | bytes 8388608 | tf_op jit(solution)/shard_map/all_to_all | solution.py:26
  21.8 0.0 all-reduce.2.cloned.1.call-start
  21.9 93.5 %all-to-all-done = bf16[16,64,2048]{2,1,0:T(8,128)(2,1)} async-done(((bf16[16,64,2048]{2,1,0:T(8,128)(2,1)}), bf16[16,64,2048]{2,1,0:T(8,128)(2,1)}, u32[]{:S(2)}, u32[]{:S(2)}) %all-to-all-start) | async-done | bytes 4194336 | tf_op jit(solution)/shard_map/all_to_all | solution.py:26
  115.4 4.4 %broadcast_select_fusion = bf16[1024,2048]{1,0:T(8,128)(2,1)} fusion(pred[]{:T(512)S(6)} %eq.3, bf16[16,64,2048]{2,1,0:T(8,128)(2,1)} %all-to-all-done), kind=kLoop, calls=%fused_computation.3 | loop fusion | flops 2097152 | bytes 8388609 | tf_op jit(solution)/shard_map/jit(_where)/select_n | solution.py:8
  119.8 0.0 all-reduce.2.cloned.1.call-update
  119.9 0.0 reduce-scatter.2.cloned.1.call-start
  119.9 3.1 multiply_reduce_fusion.1
  123.0 0.1 add.25
  123.1 199.8 %all-reduce.2.cloned.1.call-done = bf16[1024,2048]{1,0:T(8,128)(2,1)} async-done(((bf16[1024,2048]{1,0:T(8,128)(2,1)}), bf16[1024,2048]{1,0:T(8,128)(2,1)}) %all-reduce.2.cloned.1.call-update) | async-done | bytes 4194320 | tf_op jit(solution)/shard_map/psum | solution.py:9
  322.9 0.0 copy-start
  322.9 3.2 multiply_reduce_fusion
  326.1 0.2 copy-done
  326.3 8.3 %bitcast_subtract_fusion = f32[1024,1024]{0,1:T(8,128)} fusion(bf16[1024,2048]{1,0:T(8,128)(2,1)S(1)} %copy-done, bf16[1024,2048]{1,0:T(8,128)(2,1)} %bitcast, f32[1024]{0:T(1024)S(1)} %multiply_reduce_fusion, f32[1024]{0:T(1024)S(1)} %add.25), kind=kOutput, calls=%fused_computation.2 | convolution fusion | flops 4298113024 | bytes 12591104 | tf_op jit(solution)/shard_map/dot_general | solution.py:13
  334.6 0.0 reduce-scatter.2.cloned.1.call-update
  334.6 1.3 dynamic_slice.3
  336.6 63.4 %reduce-scatter.2.cloned.1.call-done = f32[512,1024]{0,1:T(8,128)} async-done(((f32[1024,1024]{0,1:T(8,128)}), f32[512,1024]{0,1:T(8,128)}) %reduce-scatter.2.cloned.1.call-update) | async-done | bytes 2097168 | tf_op jit(solution)/shard_map/reduce_scatter | solution.py:33
  400.0 1.9 multiply_convert_fusion
  401.9 1.3 copy.4
Async XLA Ops:
  10.0 105.4 %all-to-all-start = ((bf16[16,64,2048]{2,1,0:T(8,128)(2,1)}), bf16[16,64,2048]{2,1,0:T(8,128)(2,1)}, u32[]{:S(2)}, u32[]{:S(2)}) async-start(bf16[16,64,2048]{2,1,0:T(8,128)(2,1)} %stack.2), calls=%async_computation | async-start | bytes 8388608 | tf_op jit(solution)/shard_map/all_to_all | solution.py:26
  21.8 301.1 %all-reduce.2.cloned.1.call-start = ((), (), s32[]{:S(2)}) async-start(), calls=%async_computation.2 | async-start | bytes 8388608 | tf_op jit(solution)/shard_map/psum | solution.py:9
  119.9 280.1 %reduce-scatter.2.cloned.1.call-start = ((), (), s32[]{:S(2)}) async-start(), calls=%async_computation.3 | async-start | bytes 6291456 | tf_op jit(solution)/shard_map/reduce_scatter | solution.py:33
  322.9 3.4 copy-start
Sparse Core Ops, SparseCore 0:
  120.0 202.8 all-reduce.1
  334.8 65.1 reduce-scatter.1
